TPU v7x, 32 devices: a whole 2x2x4 slice. The times are simulated.
32 devices in a mesh: grp: 2 (over y), seq: 4 (over z), head: 2 (over x), rep: 2 (over core).
Axes of the slice: x: 2, y: 2, z: 4, core: 2. Of those that a mesh axis runs over, the one named last changes fastest.
Arguments:
- query_latent: bfloat16 [1024, 32, 512], P(('grp', 'seq'), ('head', 'rep')), parts along dimension 0, may hold values from -400 to 400
- query_rope: bfloat16 [1024, 2048], P(('grp', 'seq'), ('head', 'rep')), parts along dimension 0, may hold values from -4 to 4
- latent: bfloat16 [8192, 512], P(('grp', 'seq', 'rep')), parts along dimension 0, may hold values from -6 to 6
- key_rope: bfloat16 [64, 8192], P(None, ('grp', 'seq', 'rep')), parts along dimension 1, may hold values from -4 to 4
- value_up: bfloat16 [32, 512, 128], P(('head', 'rep')), may hold values from -2.390625 to 2.390625
- out_proj: bfloat16 [4096, 3584], P(('head', 'rep')), may hold values from -0.09375 to 0.09375
Outputs:
- output: bfloat16 [1024, 3584], P(('grp', 'seq', 'head', 'rep')), parts along dimension 0
There are 2 independent parts, one for each index of `grp`. A program takes and returns all parts, laid end to end along the dimension named above; an argument that names none is the same for every part. Nothing has to cross between parts.
All inputs are finite; a program needn't handle non-finite values.
Results may differ from a plain program's by a relative error of at most 0.017.
Values may be sent and summed in bfloat16 or wider, within the bound.
A program may use at most 128 MiB of HBM per device.

v0:
```python
import jax
import jax.numpy as jnp
from jax import lax
from jax.sharding import PartitionSpec as P

masked_score = -1e30


def shifted(value, axis, by):
    peers = lax.axis_size(axis)
    pairs = [(i, i + by) for i in range(peers) if 0 <= i + by < peers]
    return lax.ppermute(value, axis, pairs)


def fetch_partners(key_pair, levels):
    fetched = []
    current = key_pair
    for level_index in range(levels):
        current = shifted((key_pair[0], key_pair[1]), "seq", 2**level_index)
        fetched.append(current)
    return fetched


def attend_block(carry_state, query_latent, rope_queries, block, allowed, score_scale):
    running_max, running_sum, running_out = carry_state
    block_latent, block_rope = block
    scores = jnp.einsum(
        "qhc,kc->hqk", query_latent, block_latent, preferred_element_type=jnp.float32
    )
    scores = scores + jnp.einsum(
        "qhr,rk->hqk", rope_queries, block_rope, preferred_element_type=jnp.float32
    )
    scores = jnp.where(allowed, scores * score_scale, masked_score)
    new_max = jnp.maximum(running_max, jnp.max(scores, axis=2, keepdims=True))
    weights = jnp.exp(scores - new_max)
    factor = jnp.exp(running_max - new_max)
    running_sum = running_sum * factor + jnp.sum(weights, axis=2, keepdims=True)
    update = jnp.einsum(
        "hqk,kc->hqc",
        weights.astype(jnp.bfloat16),
        block_latent,
        preferred_element_type=jnp.float32,
    )
    return (new_max, running_sum, running_out * factor + update)


def shards(query_latent, query_rope, latent, key_rope, value_up, out_proj):
    query_rows, heads_here, latent_width = query_latent.shape
    rope_width = key_rope.shape[0]
    levels = min(4, lax.axis_size("seq") // 4 + 1)
    shard_index = lax.axis_index("seq")
    score_scale = (latent_width + rope_width) ** (-0.5)
    rope_queries = query_rope.reshape(query_rows, heads_here, rope_width)
    partners = fetch_partners((latent, key_rope), levels)
    stacked_latent = jnp.stack([latent] + [partner[0] for partner in partners])
    stacked_rope = jnp.stack([key_rope] + [partner[1] for partner in partners])
    block_latent, block_rope = (
        lax.all_gather(stacked_latent, "rep", axis=1, tiled=True),
        lax.all_gather(stacked_rope, "rep", axis=2, tiled=True),
    )
    blocks = [
        (block_latent[level_index], block_rope[level_index]) for level_index in range(levels + 1)
    ]
    block_rows = blocks[0][0].shape[0]
    key_index = jnp.arange(block_rows, dtype=jnp.int32)
    query_index = jnp.arange(query_rows, dtype=jnp.int32)
    causal = key_index[None, None, :] <= (block_rows - query_rows + query_index)[None, :, None]
    carry_state = (
        jnp.full((heads_here, query_rows, 1), masked_score, jnp.float32),
        jnp.zeros((heads_here, query_rows, 1), jnp.float32),
        jnp.zeros((heads_here, query_rows, latent_width), jnp.float32),
    )
    carry_state = attend_block(
        carry_state, query_latent, rope_queries, blocks[0], causal, score_scale
    )
    for level_index in range(levels):
        present = shard_index >= 2**level_index
        carry_state = attend_block(
            carry_state, query_latent, rope_queries, blocks[level_index + 1], present, score_scale
        )
    attended = (carry_state[2] / carry_state[1]).astype(jnp.bfloat16)
    expanded = jnp.einsum(
        "hqc,hcv->qhv", attended, value_up, preferred_element_type=jnp.float32
    ).astype(jnp.bfloat16)
    expanded = expanded.reshape(query_rows, heads_here * value_up.shape[2])
    return lax.psum_scatter(
        jnp.dot(expanded, out_proj, preferred_element_type=jnp.float32).astype(jnp.bfloat16),
        ("head", "rep"),
        scatter_dimension=0,
        tiled=True,
    )


def solution(mesh):
    placed = (
        P(("grp", "seq"), ("head", "rep"), None),
        P(("grp", "seq"), ("head", "rep")),
        P(("grp", "seq", "rep"), None),
        P(None, ("grp", "seq", "rep")),
        P(("head", "rep"), None, None),
        P(("head", "rep"), None),
    )
    return jax.shard_map(
        shards,
        mesh=mesh,
        in_specs=placed,
        out_specs=P(("grp", "seq", "head", "rep"), None),
        check_vma=False,
    )
```

profile of v0, /device:TPU:17, one launch (start us, length us, event | category | flops | bytes accessed | tf_op | source)
XLA Modules:
  0.0 118.5 jit_solution(14308483013304031724)
XLA Ops:
  6.5 1.4 %collective-permute-start.1 = (bf16[512,512]{1,0:T(8,128)(2,1)}, bf16[512,512]{1,0:T(8,128)(2,1)S(1)}, u32[]{:S(2)}, u32[]{:S(2)}) collective-permute-start(bf16[512,512]{1,0:T(8,128)(2,1)} %param.8), channel_id=1, source_target_pairs={{0,8},{4,12},{1,9},{5,13},{2,10},{6,14},{3,11},{7,15},{16,24},{20,... | collective-permute-start | bytes 1572872 | tf_op jit(solution)/shard_map/ppermute | solution.py:12
  8.0 3.2 %collective-permute-start = (bf16[512,512]{1,0:T(8,128)(2,1)}, bf16[512,512]{1,0:T(8,128)(2,1)S(1)}, u32[]{:S(2)}, u32[]{:S(2)}) collective-permute-start(bf16[512,512]{1,0:T(8,128)(2,1)} %param.8), channel_id=1, source_target_pairs={{0,4},{4,8},{8,12},{1,5},{5,9},{9,13},{2,6},{6,10},{10,14},{3,7},{... | collective-permute-start | bytes 1572872 | tf_op jit(solution)/shard_map/ppermute | solution.py:12
  11.2 11.3 %collective-permute-done.1 = bf16[512,512]{1,0:T(8,128)(2,1)S(1)} collective-permute-done((bf16[512,512]{1,0:T(8,128)(2,1)}, bf16[512,512]{1,0:T(8,128)(2,1)S(1)}, u32[]{:S(2)}, u32[]{:S(2)}) %collective-permute-start.1) | collective-permute-done | bytes 524320 | tf_op jit(solution)/shard_map/ppermute | solution.py:12
  22.5 23.5 %collective-permute-done = bf16[512,512]{1,0:T(8,128)(2,1)S(1)} collective-permute-done((bf16[512,512]{1,0:T(8,128)(2,1)}, bf16[512,512]{1,0:T(8,128)(2,1)S(1)}, u32[]{:S(2)}, u32[]{:S(2)}) %collective-permute-start) | collective-permute-done | bytes 524320 | tf_op jit(solution)/shard_map/ppermute | solution.py:12
  46.0 2.4 %pad_maximum_fusion = bf16[3,512,512]{2,1,0:T(8,128)(2,1)} fusion(bf16[1,512,512]{2,1,0:T(8,128)(2,1)S(1)} %bitcast.77, bf16[1,512,512]{2,1,0:T(8,128)(2,1)S(1)} %bitcast.78, bf16[1,512,512]{2,1,0:T(8,128)(2,1)} %bitcast.76), kind=kLoop, calls=%fused_computation.24 | loop fusion | flops 1572864 | bytes 3145728 | tf_op jit(solution)/shard_map/stack | solution.py:55
  48.5 1.3 %collective-permute-start.3 = (bf16[64,512]{1,0:T(8,128)(2,1)S(1)}, bf16[64,512]{1,0:T(8,128)(2,1)S(1)}, u32[]{:S(2)}, u32[]{:S(2)}) collective-permute-start(bf16[64,512]{1,0:T(8,128)(2,1)S(1)} %copy-done.4), channel_id=1, source_target_pairs={{0,8},{4,12},{1,9},{5,13},{2,10},{6,14},{3,11},{7,15},{16,24},{20,... | collective-permute-start | bytes 196616 | tf_op jit(solution)/shard_map/ppermute | solution.py:12
  49.8 1.9 %collective-permute-start.2 = (bf16[64,512]{1,0:T(8,128)(2,1)S(1)}, bf16[64,512]{1,0:T(8,128)(2,1)S(1)}, u32[]{:S(2)}, u32[]{:S(2)}) collective-permute-start(bf16[64,512]{1,0:T(8,128)(2,1)S(1)} %copy-done.4), channel_id=1, source_target_pairs={{0,4},{4,8},{8,12},{1,5},{5,9},{9,13},{2,6},{6,10},{10,14},{3,7},{... | collective-permute-start | bytes 196616 | tf_op jit(solution)/shard_map/ppermute | solution.py:12
  52.0 2.5 %collective-permute-done.3 = bf16[64,512]{1,0:T(8,128)(2,1)S(1)} collective-permute-done((bf16[64,512]{1,0:T(8,128)(2,1)S(1)}, bf16[64,512]{1,0:T(8,128)(2,1)S(1)}, u32[]{:S(2)}, u32[]{:S(2)}) %collective-permute-start.3) | collective-permute-done | bytes 65568 | tf_op jit(solution)/shard_map/ppermute | solution.py:12
  54.4 2.1 %collective-permute-done.2 = bf16[64,512]{1,0:T(8,128)(2,1)S(1)} collective-permute-done((bf16[64,512]{1,0:T(8,128)(2,1)S(1)}, bf16[64,512]{1,0:T(8,128)(2,1)S(1)}, u32[]{:S(2)}, u32[]{:S(2)}) %collective-permute-start.2) | collective-permute-done | bytes 65568 | tf_op jit(solution)/shard_map/ppermute | solution.py:12
  56.5 2.5 %all_gather.7 = bf16[3,64,1024]{2,1,0:T(8,128)(2,1)S(1)} all-gather(bf16[3,64,512]{2,1,0:T(8,128)(2,1)S(1)} %pad_maximum_fusion.1), channel_id=1, replica_groups=mesh['grp'=2,'seq'=4,'head'=2,'rep'=2] {'rep'}, dimensions={2}, use_global_device_ids=true | all-gather | bytes 589824 | tf_op jit(solution)/shard_map/all_gather | solution.py:59
  59.0 2.3 %all-gather.2.cloned.1.call-done = bf16[3,1024,512]{2,1,0:T(8,128)(2,1)} async-done(((bf16[3,512,512]{2,1,0:T(8,128)(2,1)}), bf16[3,1024,512]{2,1,0:T(8,128)(2,1)}) %all-gather.2.cloned.1.call-update) | async-done | bytes 3145744 | tf_op jit(solution)/shard_map/all_gather | solution.py:58
  61.3 2.6 %fusion.31 = f32[1024,128,8]{1,0,2:T(8,128)S(1)} fusion(bf16[3,1024,512]{2,1,0:T(8,128)(2,1)} %all-gather.2.cloned.1.call-done, bf16[128,8,512]{2,1,0:T(8,128)(2,1)S(1)} %copy-done), kind=kOutput, calls=%fused_computation.36 | convolution fusion | flops 1073741824 | bytes 6291456 | tf_op jit(solution)/shard_map/qhc,kc->hqk/dot_general | solution.py:27
  63.9 0.8 bitcast_reduce_fusion
  64.7 1.1 copy-done.2
  65.8 1.4 %fusion.30 = f32[1024,128,8]{1,0,2:T(8,128)S(1)} fusion(bf16[3,1024,512]{2,1,0:T(8,128)(2,1)S(1)} %copy-done.2, bf16[128,8,512]{2,1,0:T(8,128)(2,1)S(1)} %copy-done), kind=kOutput, calls=%fused_computation.35 | convolution fusion | flops 1073741824 | bytes 6291456 | tf_op jit(solution)/shard_map/qhc,kc->hqk/dot_general | solution.py:27
  67.2 0.8 bitcast_reduce_fusion.1
  68.0 1.4 %fusion.29 = f32[1024,128,8]{1,0,2:T(8,128)S(1)} fusion(bf16[3,1024,512]{2,1,0:T(8,128)(2,1)S(1)} %copy-done.2, bf16[128,8,512]{2,1,0:T(8,128)(2,1)S(1)} %copy-done), kind=kOutput, calls=%fused_computation.34 | convolution fusion | flops 1073741824 | bytes 6291456 | tf_op jit(solution)/shard_map/qhc,kc->hqk/dot_general | solution.py:27
  69.4 1.0 fusion.38
  71.0 1.1 fusion.2
  72.4 1.3 %fusion.8 = f32[8,128,512]{2,1,0:T(8,128)S(1)} fusion(f32[1024,128,8]{1,0,2:T(8,128)S(1)} %get-tuple-element.13, f32[8,128]{1,0:T(8,128)S(1)} %get-tuple-element.8, bf16[3,1024,512]{2,1,0:T(8,128)(2,1)S(1)} %copy-done.2), kind=kOutput, calls=%fused_computation.17 | convolution fusion | flops 1075838976 | bytes 7344128 | tf_op jit(solution)/shard_map/hqk,kc->hqc/dot_general | solution.py:38
  73.7 2.7 %fusion.10 = f32[8,128,512]{2,1,0:T(8,128)} fusion(f32[1024,128,8]{1,0,2:T(8,128)S(1)} %get-tuple-element.15, f32[8,128]{1,0:T(8,128)S(1)} %get-tuple-element.9, bf16[3,1024,512]{2,1,0:T(8,128)(2,1)S(1)} %copy-done.2), kind=kOutput, calls=%fused_computation.18 | convolution fusion | flops 1075838976 | bytes 7344128 | tf_op jit(solution)/shard_map/hqk,kc->hqc/dot_general | solution.py:38
  76.4 5.4 %fusion.22 = bf16[8,128,128]{1,2,0:T(8,128)(2,1)S(1)} fusion(bf16[8,512,128]{2,1,0:T(8,128)(2,1)} %param.10, f32[8,128,512]{2,1,0:T(8,128)S(1)} %fusion.8, f32[8,128,512]{2,1,0:T(8,128)} %fusion.10, f32[8,128,1024]{1,2,0:T(8,128)} %copy-done.1, f32[8,128]{1,0:T(8,128)S(1)} %get-tuple-element.11, f32[8,128]{1,0:T(8,128)S(1)} %get-tuple-element.5, ...), kind=kOutput, calls=%fused_computation.26 | convolution fusion | flops 1213857792 | bytes 10768384 | tf_op jit(solution)/shard_map/hqc,hcv->qhv/dot_general | solution.py:82
  81.8 5.2 %convolution_convert_fusion = bf16[128,3584]{1,0:T(8,128)(2,1)} fusion(bf16[128,1024]{0,1:T(8,128)(2,1)S(1)} %bitcast.75, bf16[1024,3584]{1,0:T(8,128)(2,1)} %param.11), kind=kOutput, calls=%fused_computation | convolution fusion | flops 939982848 | bytes 8519680 | tf_op jit(solution)/shard_map/dot_general | solution.py:87
  86.9 24.7 %reduce-scatter.2.cloned.1.call-done = bf16[32,3584]{1,0:T(8,128)(2,1)} async-done(((bf16[128,3584]{1,0:T(8,128)(2,1)}), bf16[32,3584]{1,0:T(8,128)(2,1)}) %reduce-scatter.2.cloned.1.call-update) | async-done | bytes 229392 | tf_op jit(solution)/shard_map/reduce_scatter | solution.py:86
  (20 shorter events, 1.1 us)
Async XLA Ops:
  6.5 54.8 %copy-start = (bf16[128,8,512]{2,1,0:T(8,128)(2,1)S(1)}, bf16[128,8,512]{2,1,0:T(8,128)(2,1)}, u32[]{:S(2)}) copy-start(bf16[128,8,512]{2,1,0:T(8,128)(2,1)} %param.6) | copy-start | bytes 3145732
  6.5 42.0 %copy-start.4 = (bf16[64,512]{1,0:T(8,128)(2,1)S(1)}, bf16[64,512]{1,0:T(8,128)(2,1)}, u32[]{:S(2)}) copy-start(bf16[64,512]{1,0:T(8,128)(2,1)} %param.9) | copy-start | bytes 196612
  6.5 45.3 %copy-start.3 = (bf16[128,512]{1,0:T(8,128)(2,1)S(1)}, bf16[128,512]{1,0:T(8,128)(2,1)}, u32[]{:S(2)}) copy-start(bf16[128,512]{1,0:T(8,128)(2,1)} %param.7) | copy-start | bytes 393220
  6.5 54.8 %all-gather.2.cloned.1.call-start = ((), (), s32[]{:S(2)}) async-start(), calls=%async_computation.1 | async-start | bytes 4718592 | tf_op jit(solution)/shard_map/all_gather | solution.py:58
  6.5 16.0 %collective-permute-start.1 = (bf16[512,512]{1,0:T(8,128)(2,1)}, bf16[512,512]{1,0:T(8,128)(2,1)S(1)}, u32[]{:S(2)}, u32[]{:S(2)}) collective-permute-start(bf16[512,512]{1,0:T(8,128)(2,1)} %param.8), channel_id=1, source_target_pairs={{0,8},{4,12},{1,9},{5,13},{2,10},{6,14},{3,11},{7,15},{16,24},{20,... | collective-permute-start | bytes 1572872 | tf_op jit(solution)/shard_map/ppermute | solution.py:12
  8.0 38.1 %collective-permute-start = (bf16[512,512]{1,0:T(8,128)(2,1)}, bf16[512,512]{1,0:T(8,128)(2,1)S(1)}, u32[]{:S(2)}, u32[]{:S(2)}) collective-permute-start(bf16[512,512]{1,0:T(8,128)(2,1)} %param.8), channel_id=1, source_target_pairs={{0,4},{4,8},{8,12},{1,5},{5,9},{9,13},{2,6},{6,10},{10,14},{3,7},{... | collective-permute-start | bytes 1572872 | tf_op jit(solution)/shard_map/ppermute | solution.py:12
  48.4 63.2 %reduce-scatter.2.cloned.1.call-start = ((), (), s32[]{:S(2)}) async-start(), calls=%async_computation.2 | async-start | bytes 1146880 | tf_op jit(solution)/shard_map/reduce_scatter | solution.py:86
  48.5 5.9 %collective-permute-start.3 = (bf16[64,512]{1,0:T(8,128)(2,1)S(1)}, bf16[64,512]{1,0:T(8,128)(2,1)S(1)}, u32[]{:S(2)}, u32[]{:S(2)}) collective-permute-start(bf16[64,512]{1,0:T(8,128)(2,1)S(1)} %copy-done.4), channel_id=1, source_target_pairs={{0,8},{4,12},{1,9},{5,13},{2,10},{6,14},{3,11},{7,15},{16,24},{20,... | collective-permute-start | bytes 196616 | tf_op jit(solution)/shard_map/ppermute | solution.py:12
  49.8 6.7 %collective-permute-start.2 = (bf16[64,512]{1,0:T(8,128)(2,1)S(1)}, bf16[64,512]{1,0:T(8,128)(2,1)S(1)}, u32[]{:S(2)}, u32[]{:S(2)}) collective-permute-start(bf16[64,512]{1,0:T(8,128)(2,1)S(1)} %copy-done.4), channel_id=1, source_target_pairs={{0,4},{4,8},{8,12},{1,5},{5,9},{9,13},{2,6},{6,10},{10,14},{3,7},{... | collective-permute-start | bytes 196616 | tf_op jit(solution)/shard_map/ppermute | solution.py:12
  63.9 1.9 %copy-start.2 = (bf16[3,1024,512]{2,1,0:T(8,128)(2,1)S(1)}, bf16[3,1024,512]{2,1,0:T(8,128)(2,1)}, u32[]{:S(2)}) copy-start(bf16[3,1024,512]{2,1,0:T(8,128)(2,1)} %all-gather.2.cloned.1.call-done) | copy-start | bytes 9437188
  70.4 1.9 %copy-start.1 = (f32[8,128,1024]{1,2,0:T(8,128)}, f32[8,128,1024]{1,2,0:T(8,128)S(1)}, u32[]{:S(2)}) copy-start(f32[8,128,1024]{1,2,0:T(8,128)S(1)} %get-tuple-element.17) | copy-start | bytes 12582916
Sparse Core Ops, SparseCore 0:
  48.6 12.7 all-gather.1
  87.1 24.5 reduce-scatter.1
where the time goes:
time: 120 us; the launch traced here: 118 us
  waiting for transfers between devices  66.4 us (55%)
  matrix products  22.5 us (19%)
  between operations  13.6 us (11%)
  starting transfers between devices  7.88 us (7%)
  other arithmetic  4.19 us (3%)
  blocking collectives  2.5 us (2%)
  local copies, waits for them, and re-layouts  1.43 us (1%)
    ppermute x4, waiting for transfers between devices, shifted(): return lax.ppermute(value, axis, pairs)  39.4 us
    reduce_scatter x1, waiting for transfers between devices, shards(): lax.psum_scatter(jnp.dot(expanded, out_proj, preferred_element_type=jnp.f...  24.7 us
    ppermute x4, starting transfers between devices, shifted(): return lax.ppermute(value, axis, pairs)  7.84 us
    dot_general x3, matrix products, attend_block(): jnp.einsum('qhc,kc->hqk', query_latent, block_latent, preferred_element_t...  5.41 us
    dot_general x1, matrix products, shards(): jnp.einsum('hqc,hcv->qhv', attended, value_up, preferred_element_type=jnp...  5.4 us
    dot_general x1, matrix products, shards(): jnp.dot(expanded, out_proj, preferred_element_type=jnp.float32)  5.16 us
    dot_general x2, matrix products, attend_block(): jnp.einsum('hqk,kc->hqc', weights.astype(jnp.bfloat16), block_latent, pre...  3.97 us
    dot_general x3, matrix products, attend_block(): jnp.einsum('qhr,rk->hqk', rope_queries, block_rope, preferred_element_typ...  2.57 us
  transfers between devices with their start and end apart: 6, of which 6 were waited for; matrix products, arithmetic and copies ran while one was open for 0% of the time, Pallas kernels for 0%

commit v1 on v0

v1 whole, which is shorter than its diff:
```python
import functools
import math

import jax
import jax.numpy as jnp
from jax import lax
from jax.experimental import pallas as pl
from jax.experimental.pallas import tpu as pltpu
from jax.sharding import PartitionSpec as P

lanes = 128
masked_score = -1e30
MESH = pl.DeviceIdType.MESH


def tile_rows(rows, most):
    tile = min(rows, most)
    while rows % tile:
        tile -= 8
    return tile


def column_width(columns, most):
    width = most
    while columns % width:
        width -= lanes
    return width


def kernel(
    dims,
    query_hbm,
    query_rope_hbm,
    latent_hbm,
    rope_hbm,
    value_up_hbm,
    out_proj_hbm,
    out_ref,
    keys,
    query_in,
    query_rope_in,
    rope_in,
    value_up,
    out_proj,
    queries,
    rope_wide,
    rope_queries,
    row_max,
    row_sum,
    attended,
    expanded,
    partial,
    core_out,
    core_in,
    head_out,
    head_in,
    local_sem,
    own_send,
    own_recv,
    seq_send,
    seq_recv,
    head_send,
    head_recv,
    core_send,
    core_recv,
    sum_core_send,
    sum_core_recv,
    sum_head_send,
    sum_head_recv,
):
    n_seq, n_head, levels, heads, q_dev, width, rope_width, chunk, per_share = dims
    rows = q_dev * heads
    half = latent_hbm.shape[0]
    chunks = half // chunk
    pack = keys.shape[3] - chunk
    z = lax.axis_index("seq")
    x = lax.axis_index("head")
    c = lax.axis_index("rep")
    sibling = 1 - c
    scale = (width + rope_width) ** (-0.5) * math.log2(math.e)

    latent_loads = [
        pltpu.make_async_copy(
            latent_hbm.at[pl.ds(j * chunk, chunk), :],
            keys.at[0, c, j, pl.ds(0, chunk), :],
            local_sem.at[j],
        )
        for j in range(chunks)
    ]
    rope_load = pltpu.make_async_copy(rope_hbm, rope_in, local_sem.at[chunks])
    query_load = pltpu.make_async_copy(query_hbm, query_in, local_sem.at[chunks + 1])
    query_rope_load = pltpu.make_async_copy(
        query_rope_hbm, query_rope_in, local_sem.at[chunks + 2]
    )
    value_load = pltpu.make_async_copy(value_up_hbm, value_up, local_sem.at[chunks + 3])
    proj_load = pltpu.make_async_copy(out_proj_hbm, out_proj, local_sem.at[chunks + 4])
    rope_load.start()
    for load in latent_loads:
        load.start()
    query_load.start()
    query_rope_load.start()

    hops = sorted({1} | {2 ** (b - 1) for b in range(1, levels)})
    barrier = pltpu.get_barrier_semaphore()
    pl.semaphore_signal(barrier, inc=1, device_id={"rep": sibling}, device_id_type=MESH)
    for k in range(1, n_head):
        pl.semaphore_signal(
            barrier, inc=1, device_id={"head": lax.rem(x + k, n_head)}, device_id_type=MESH
        )
    for hop in hops:

        @pl.when(z >= hop)
        def _():
            pl.semaphore_signal(
                barrier, inc=1, device_id={"seq": z - hop}, device_id_type=MESH
            )

    rope_load.wait()
    for load in latent_loads:
        load.wait()
    value_load.start()
    proj_load.start()
    per_row = width // chunk
    for j in range(chunks):
        for k in range(per_row):
            keys[0, c, j, chunk : chunk + pack, k * chunk : (k + 1) * chunk] = rope_in[
                k * pack : (k + 1) * pack, j * chunk : (j + 1) * chunk
            ]

    targets = n_head
    for hop in hops:
        targets = targets + jnp.where(z + hop < n_seq, 1, 0)
    pl.semaphore_wait(barrier, targets)

    def share(k):
        return lax.rem(x + n_head - k, n_head)

    def place(b, r, k, i):
        return keys.at[b, r, share(k) * per_share + i]

    def seq_copy(b, i):
        hop = 1 if b == 1 else 2 ** (b - 2)
        return pltpu.make_async_remote_copy(
            src_ref=place(b - 1, c, 0, i),
            dst_ref=place(b, c, 0, i),
            send_sem=seq_send.at[b - 1, i],
            recv_sem=seq_recv.at[b - 1, i],
            device_id={"seq": jnp.minimum(z + hop, n_seq - 1)},
            device_id_type=MESH,
        )

    def seq_start(b, i):
        hop = 1 if b == 1 else 2 ** (b - 2)
        return (z + hop < n_seq) & (z >= (0 if b == 1 else 2 ** (b - 2)))

    def head_copy(b, k, i):
        return pltpu.make_async_remote_copy(
            src_ref=place(b, c, 0, i),
            dst_ref=place(b, c, 0, i),
            send_sem=head_send.at[b - 1, k - 1, i],
            recv_sem=head_recv.at[b - 1, k - 1, i],
            device_id={"head": lax.rem(x + k, n_head)},
            device_id_type=MESH,
        )

    def head_arrival(b, k, i):
        return pltpu.make_async_remote_copy(
            src_ref=place(b, c, k, i),
            dst_ref=place(b, c, k, i),
            send_sem=head_send.at[b - 1, k - 1, i],
            recv_sem=head_recv.at[b - 1, k - 1, i],
            device_id={"head": lax.rem(x + k, n_head)},
            device_id_type=MESH,
        )

    def core_copy(b, k, i, r):
        return pltpu.make_async_remote_copy(
            src_ref=place(b, r, k, i),
            dst_ref=place(b, r, k, i),
            send_sem=core_send.at[b - 1, k, i],
            recv_sem=core_recv.at[b - 1, k, i],
            device_id={"rep": sibling},
            device_id_type=MESH,
        )

    def own_copy(r):
        return pltpu.make_async_remote_copy(
            src_ref=keys.at[0, r],
            dst_ref=keys.at[0, r],
            send_sem=own_send,
            recv_sem=own_recv,
            device_id={"rep": sibling},
            device_id_type=MESH,
        )

    def send_on(b, i):
        @pl.when(z >= 2 ** (b - 1))
        def _():
            seq_copy(b, i).wait_recv()
            if b < levels:

                @pl.when(seq_start(b + 1, i))
                def _():
                    seq_copy(b + 1, i).start()

            for k in range(1, n_head):
                head_copy(b, k, i).start()
            core_copy(b, 0, i, c).start()

    def pass_core(b, k, i):
        @pl.when(z >= 2 ** (b - 1))
        def _():
            head_arrival(b, k, i).wait_recv()
            core_copy(b, k, i, c).start()

    for i in range(per_share):

        @pl.when(seq_start(1, i))
        def _():
            seq_copy(1, i).start()

    own_copy(c).start()

    query_load.wait()
    query_rope_load.wait()
    if len(query_in.shape) == 3:
        step_q = q_dev // 4
        for part in range(4):
            queries[part * step_q * heads : (part + 1) * step_q * heads, :] = (
                query_in[part * step_q : (part + 1) * step_q]
                .astype(jnp.float32)
                .reshape(step_q * heads, width)
                .astype(jnp.bfloat16)
            )
        query_source = queries
    else:
        query_source = query_in
    for h in range(heads):
        start = h * rope_width // lanes * lanes
        shift = h * rope_width - start
        piece = query_rope_in[:, start : start + lanes].astype(jnp.float32)
        if shift:
            piece = pltpu.roll(piece, lanes - shift, 1)
        rope_wide[pl.ds(h, q_dev, stride=heads), :] = piece
    rope_queries[...] = rope_wide[:, :rope_width].astype(jnp.bfloat16)

    tile = tile_rows(rows, 256)

    def attend(places, first=False, key_base=None):
        def key_rows():
            return jnp.concatenate([keys[b, r, j, :chunk, :] for b, r, j in places], axis=0)

        def key_ropes():
            return jnp.concatenate(
                [
                    jnp.concatenate(
                        [
                            keys[b, r, j, chunk : chunk + pack, k * chunk : (k + 1) * chunk]
                            for k in range(per_row)
                        ],
                        axis=0,
                    )
                    for b, r, j in places
                ],
                axis=1,
            )

        def scores_of(base):
            at = pl.ds(base, tile)
            scores = lax.dot_general(
                query_source[at, :],
                key_rows(),
                (((1,), (1,)), ((), ())),
                preferred_element_type=jnp.float32,
            )
            scores = scores + jnp.dot(
                rope_queries[at, :], key_ropes(), preferred_element_type=jnp.float32
            )
            if key_base is not None:
                key = key_base + lax.broadcasted_iota(jnp.int32, scores.shape, 1)
                row = base + lax.broadcasted_iota(jnp.int32, scores.shape, 0)
                limit = (2 * half - q_dev) + row // heads
                scores = jnp.where(key <= limit, scores, masked_score)
            return scores * scale

        def fold(base, scores):
            at = pl.ds(base, tile)
            top = jnp.max(scores, axis=1, keepdims=True)
            if not first:
                old = row_max[at, :1]
                top = jnp.maximum(top, old)
            weights = jnp.exp2(scores - top)
            part = weights[:, :lanes]
            for k in range(1, weights.shape[1] // lanes):
                part = part + weights[:, k * lanes : (k + 1) * lanes]
            update = jnp.dot(
                weights.astype(jnp.bfloat16), key_rows(), preferred_element_type=jnp.float32
            )
            if first:
                row_sum[at, :] = part
            else:
                factor = jnp.exp2(old - top)
                row_sum[at, :] = row_sum[at, :] * factor + part
            for k in range(width // lanes):
                piece = update[:, k * lanes : (k + 1) * lanes]
                if not first:
                    piece = attended[k, at, :] * factor + piece
                attended[k, at, :] = piece
            row_max[at, :] = jnp.broadcast_to(top, (tile, lanes))

        def body(step, _):
            base = pl.multiple_of(step * (2 * tile), tile)
            left = scores_of(base)
            right = scores_of(base + tile)
            fold(base, left)
            fold(base + tile, right)
            return 0

        lax.fori_loop(0, rows // (2 * tile), body, 0)

    def attend_share(b, k):
        @pl.when(z >= 2 ** (b - 1))
        def _():
            for i in range(per_share):
                core_copy(b, k, i, sibling).wait_recv()
            attend(
                [
                    (b, r, share(k) * per_share + i)
                    for r in (c, sibling)
                    for i in range(per_share)
                ]
            )

    attend([(0, c, j) for j in range(chunks)], first=True, key_base=c * half)
    send_on(1, 0)
    own_copy(sibling).wait_recv()
    attend([(0, sibling, j) for j in range(chunks)], key_base=sibling * half)
    for i in range(1, per_share):
        send_on(1, i)
    for b in range(1, levels + 1):
        for k in range(1, n_head):
            pass_core(b, k, 0)
        attend_share(b, 0)
        if b < levels:
            send_on(b + 1, 0)
        for k in range(1, n_head):
            for i in range(1, per_share):
                pass_core(b, k, i)
        for k in range(1, n_head):
            attend_share(b, k)
        if b < levels:
            for i in range(1, per_share):
                send_on(b + 1, i)

    value_load.wait()

    def normalise(step, _):
        at = pl.ds(pl.multiple_of(step * tile, tile), tile)
        inverse = 1.0 / jnp.sum(row_sum[at, :], axis=1, keepdims=True)
        for k in range(width // lanes):
            attended[k, at, :] = attended[k, at, :] * inverse
        return 0

    lax.fori_loop(0, rows // tile, normalise, 0)
    value_width = value_up.shape[2]
    for h in range(heads):
        latent_out = jnp.concatenate(
            [
                attended[k, pl.ds(h, q_dev, stride=heads), :].astype(jnp.bfloat16)
                for k in range(width // lanes)
            ],
            axis=1,
        )
        expanded[:, h * value_width : (h + 1) * value_width] = jnp.dot(
            latent_out, value_up[h], preferred_element_type=jnp.float32
        ).astype(jnp.bfloat16)

    proj_load.wait()
    columns, out_rows = core_out.shape[3], core_out.shape[2]
    pieces = core_out.shape[0]

    def sum_core(piece):
        return pltpu.make_async_remote_copy(
            src_ref=core_out.at[piece],
            dst_ref=core_in.at[piece],
            send_sem=sum_core_send.at[piece],
            recv_sem=sum_core_recv.at[piece],
            device_id={"rep": sibling},
            device_id_type=MESH,
        )

    def sum_head(piece, k):
        return pltpu.make_async_remote_copy(
            src_ref=head_out.at[piece, k - 1],
            dst_ref=head_in.at[piece, k - 1],
            send_sem=sum_head_send.at[piece, k - 1],
            recv_sem=sum_head_recv.at[piece, k - 1],
            device_id={"head": lax.rem(x + k, n_head)},
            device_id_type=MESH,
        )

    def project(piece):
        product = jnp.dot(
            expanded[...],
            out_proj[:, piece * columns : (piece + 1) * columns],
            preferred_element_type=jnp.float32,
        )
        partial[piece] = product.reshape(n_head * 2, out_rows, columns)
        for k in range(n_head):
            core_out[piece, k] = partial[
                piece, lax.rem(x + k, n_head) * 2 + sibling
            ].astype(jnp.bfloat16)
        sum_core(piece).start()

    def add_core(piece):
        sum_core(piece).wait_recv()
        for k in range(1, n_head):
            head_out[piece, k - 1] = (
                partial[piece, lax.rem(x + k, n_head) * 2 + c]
                + core_in[piece, k].astype(jnp.float32)
            ).astype(jnp.bfloat16)
            sum_head(piece, k).start()

    for piece in range(pieces):
        project(piece)
        if piece:
            add_core(piece - 1)
    add_core(pieces - 1)
    for piece in range(pieces):
        total = partial[piece, x * 2 + c] + core_in[piece, 0].astype(jnp.float32)
        for k in range(1, n_head):
            sum_head(piece, k).wait_recv()
            total = total + head_in[piece, k - 1].astype(jnp.float32)
        out_ref[:, piece * columns : (piece + 1) * columns] = total.astype(out_ref.dtype)

    own_copy(c).wait_send()
    for b in range(1, levels + 1):
        for i in range(per_share):

            @pl.when(seq_start(b, i))
            def _():
                seq_copy(b, i).wait_send()

            @pl.when(z >= 2 ** (b - 1))
            def _():
                for k in range(1, n_head):
                    head_copy(b, k, i).wait_send()
                for k in range(n_head):
                    core_copy(b, k, i, c).wait_send()

    for piece in range(pieces):
        sum_core(piece).wait_send()
        for k in range(1, n_head):
            sum_head(piece, k).wait_send()


def shards(query_latent, query_rope, latent, key_rope, value_up, out_proj):
    q_dev, heads, width = query_latent.shape
    rope_width = key_rope.shape[0]
    half = latent.shape[0]
    n_seq, n_head = lax.axis_size("seq"), lax.axis_size("head")
    levels = min(4, n_seq // 4 + 1)
    chunk = lanes
    per_share = half // (n_head * chunk)
    chunks = half // chunk
    pack = rope_width * chunk // width
    rows = q_dev * heads
    features = out_proj.shape[1]
    columns = column_width(features, 8 * lanes)
    pieces = features // columns
    out_rows = q_dev // (2 * n_head)
    dims = (n_seq, n_head, levels, heads, q_dev, width, rope_width, chunk, per_share)
    if heads % 8:
        query_latent = query_latent.reshape(rows, width)
    bf16, f32 = jnp.bfloat16, jnp.float32
    dma = pltpu.SemaphoreType.DMA
    others = max(1, n_head - 1)
    return pl.pallas_call(
        functools.partial(kernel, dims),
        out_shape=jax.ShapeDtypeStruct((out_rows, features), bf16),
        in_specs=[pl.BlockSpec(memory_space=pl.ANY)] * 6,
        out_specs=pl.BlockSpec(memory_space=pltpu.VMEM),
        scratch_shapes=[
            pltpu.VMEM((levels + 1, 2, chunks, chunk + pack, width), bf16),
            pltpu.VMEM(query_latent.shape, bf16),
            pltpu.VMEM(query_rope.shape, bf16),
            pltpu.VMEM(key_rope.shape, bf16),
            pltpu.VMEM(value_up.shape, bf16),
            pltpu.VMEM(out_proj.shape, bf16),
            pltpu.VMEM((rows, width), bf16),
            pltpu.VMEM((rows, lanes), f32),
            pltpu.VMEM((rows, rope_width), bf16),
            pltpu.VMEM((rows, lanes), f32),
            pltpu.VMEM((rows, lanes), f32),
            pltpu.VMEM((width // lanes, rows, lanes), f32),
            pltpu.VMEM((q_dev, heads * value_up.shape[2]), bf16),
            pltpu.VMEM((pieces, 2 * n_head, out_rows, columns), f32),
            pltpu.VMEM((pieces, n_head, out_rows, columns), bf16),
            pltpu.VMEM((pieces, n_head, out_rows, columns), bf16),
            pltpu.VMEM((pieces, others, out_rows, columns), bf16),
            pltpu.VMEM((pieces, others, out_rows, columns), bf16),
            dma((chunks + 5,)),
            dma,
            dma,
            dma((levels, per_share)),
            dma((levels, per_share)),
            dma((levels, others, per_share)),
            dma((levels, others, per_share)),
            dma((levels, n_head, per_share)),
            dma((levels, n_head, per_share)),
            dma((pieces,)),
            dma((pieces,)),
            dma((pieces, others)),
            dma((pieces, others)),
        ],
        compiler_params=pltpu.CompilerParams(
            collective_id=0, has_side_effects=True, vmem_limit_bytes=50 * 1024 * 1024
        ),
        cost_estimate=pl.CostEstimate(
            flops=2 * rows * (levels + 1) * 2 * half * (2 * width + rope_width),
            bytes_accessed=2 * (rows * width + out_proj.size),
            transcendentals=rows * (levels + 1) * 2 * half,
        ),
    )(query_latent, query_rope, latent, key_rope, value_up, out_proj)


def solution(mesh):
    placed = (
        P(("grp", "seq"), ("head", "rep"), None),
        P(("grp", "seq"), ("head", "rep")),
        P(("grp", "seq", "rep"), None),
        P(None, ("grp", "seq", "rep")),
        P(("head", "rep"), None, None),
        P(("head", "rep"), None),
    )
    return jax.shard_map(
        shards,
        mesh=mesh,
        in_specs=placed,
        out_specs=P(("grp", "seq", "head", "rep"), None),
        check_vma=False,
    )
```

time: 120 us -> 43.3 us (0.36); the launches traced: 118 us -> 43 us
  waiting for transfers between devices: 66.4 us -> 0 us
  Pallas kernels: 0 us -> 37 us
  matrix products: 22.5 us -> 0 us
  between operations: 13.6 us -> 0.01 us
  starting transfers between devices: 7.88 us -> 0 us
  local copies, waits for them, and re-layouts: 1.43 us -> 5.92 us
  other arithmetic: 4.19 us -> 0 us
  blocking collectives: 2.5 us -> 0 us
    ppermute x4 -> x0, waiting for transfers between devices: 39.4 us -> none  [shifted(): return lax.ppermute(value, axis, pairs)]
    pallas_call x0 -> x1, Pallas kernels: none -> 37 us  [shards(): pl.pallas_call(functools.partial(kernel, dims), out_shape=jax.ShapeDtypeS...]
    reduce_scatter x1 -> x0, waiting for transfers between devices: 24.7 us -> none  [shards(): lax.psum_scatter(jnp.dot(expanded, out_proj, preferred_element_type=jnp.f...]
    dot_general x10 -> x0, matrix products: 22.5 us -> none  [the longest x3 5.41 us: attend_block(): jnp.einsum('qhc,kc->hqk', query_latent, block_latent, preferred_element_t...]
    ppermute x4 -> x0, starting transfers between devices: 7.84 us -> none  [shifted(): return lax.ppermute(value, axis, pairs)]
    unnamed x11, local copies, waits for them, and re-layouts: 1.43 us -> 5.92 us
    all_gather x1 -> x0, blocking collectives: 2.5 us -> none  [shards(): lax.all_gather(stacked_rope, 'rep', axis=2, tiled=True)]
    another operation x2 -> x0, other arithmetic: 2.39 us -> none  [the longest x1 2.37 us: shards(): stacked_latent = jnp.stack([latent] + [partner[0] for partner in partners])]
  transfers between devices with their start and end apart: 6 -> 0, of which waited for: 6 -> 0; matrix products, arithmetic and copies ran while one was open for 0% -> 0% of each run, Pallas kernels for 0% -> 0%
where the time goes in v1:
time: 43.3 us; the launch traced here: 43 us
  Pallas kernels  37 us (85%)
  local copies, waits for them, and re-layouts  5.92 us (14%)
    pallas_call x1, Pallas kernels, shards(): pl.pallas_call(functools.partial(kernel, dims), out_shape=jax.ShapeDtypeS...  37 us
    unnamed x11, local copies, waits for them, and re-layouts  5.92 us

profile of v1, /device:TPU:17, one launch (start us, length us, event | category | flops | bytes accessed | tf_op | source)
XLA Modules:
  0.0 43.0 jit_solution(11447675342284359023)
XLA Ops:
  0.0 0.0 copy-start
  0.0 1.2 %copy-done = bf16[128,8,512]{2,1,0:T(8,128)(2,1)S(1)} copy-done((bf16[128,8,512]{2,1,0:T(8,128)(2,1)S(1)}, bf16[128,8,512]{2,1,0:T(8,128)(2,1)}, u32[]{:S(2)}) %copy-start) | copy-done | bytes 1048600
  1.2 0.0 copy-start.1
  1.2 1.2 %copy-done.1 = bf16[8,512,128]{2,1,0:T(8,128)(2,1)S(1)} copy-done((bf16[8,512,128]{2,1,0:T(8,128)(2,1)S(1)}, bf16[8,512,128]{2,1,0:T(8,128)(2,1)}, u32[]{:S(2)}) %copy-start.1) | copy-done | bytes 1048600
  2.5 0.0 copy-start.2
  2.5 1.0 %copy-done.2 = bf16[512,512]{1,0:T(8,128)(2,1)S(1)} copy-done((bf16[512,512]{1,0:T(8,128)(2,1)S(1)}, bf16[512,512]{1,0:T(8,128)(2,1)}, u32[]{:S(2)}) %copy-start.2) | copy-done | bytes 524312
  3.5 0.0 copy-start.3
  3.5 0.9 %copy-done.3 = bf16[128,512]{1,0:T(8,128)(2,1)S(1)} copy-done((bf16[128,512]{1,0:T(8,128)(2,1)S(1)}, bf16[128,512]{1,0:T(8,128)(2,1)}, u32[]{:S(2)}) %copy-start.3) | copy-done | bytes 131096
  4.4 0.0 copy-start.4
  4.4 0.8 %copy-done.4 = bf16[64,512]{1,0:T(8,128)(2,1)S(1)} copy-done((bf16[64,512]{1,0:T(8,128)(2,1)S(1)}, bf16[64,512]{1,0:T(8,128)(2,1)}, u32[]{:S(2)}) %copy-start.4) | copy-done | bytes 65560
  5.2 37.0 %shard_map.64 = bf16[32,3584]{1,0:T(8,128)(2,1)S(1)} custom-call(bf16[128,8,512]{2,1,0:T(8,128)(2,1)S(1)} %copy-done, bf16[128,512]{1,0:T(8,128)(2,1)S(1)} %copy-done.3, bf16[512,512]{1,0:T(8,128)(2,1)S(1)} %copy-done.2, bf16[64,512]{1,0:T(8,128)(2,1)S(1)} %copy-done.4, bf16[8,512,128]{2,1,0:T(8,128)(2,1)S(1)} %copy-done.1, bf16[1024,3584]{1,0:T(8,128)(2,1)} %out_proj_hbm.1), custom_call_target="tpu_custom_call" | custom-call | flops 6845104128 | bytes 8388608 | tf_op jit(solution)/shard_map/pallas_call | solution.py:478
  42.3 0.7 %copy.8 = bf16[32,3584]{1,0:T(8,128)(2,1)} copy(bf16[32,3584]{1,0:T(8,128)(2,1)S(1)} %shard_map.64) | data formatting | bytes 458752
Async XLA Ops:
  0.0 1.2 %copy-start = (bf16[128,8,512]{2,1,0:T(8,128)(2,1)S(1)}, bf16[128,8,512]{2,1,0:T(8,128)(2,1)}, u32[]{:S(2)}) copy-start(bf16[128,8,512]{2,1,0:T(8,128)(2,1)} %query_hbm.1) | copy-start | bytes 3145732
  1.2 1.2 %copy-start.1 = (bf16[8,512,128]{2,1,0:T(8,128)(2,1)S(1)}, bf16[8,512,128]{2,1,0:T(8,128)(2,1)}, u32[]{:S(2)}) copy-start(bf16[8,512,128]{2,1,0:T(8,128)(2,1)} %value_up_hbm.1) | copy-start | bytes 3145732
  2.5 1.0 %copy-start.2 = (bf16[512,512]{1,0:T(8,128)(2,1)S(1)}, bf16[512,512]{1,0:T(8,128)(2,1)}, u32[]{:S(2)}) copy-start(bf16[512,512]{1,0:T(8,128)(2,1)} %latent_hbm.1) | copy-start | bytes 1572868
  3.5 0.9 %copy-start.3 = (bf16[128,512]{1,0:T(8,128)(2,1)S(1)}, bf16[128,512]{1,0:T(8,128)(2,1)}, u32[]{:S(2)}) copy-start(bf16[128,512]{1,0:T(8,128)(2,1)} %query_rope_hbm.1) | copy-start | bytes 393220
  4.4 0.8 %copy-start.4 = (bf16[64,512]{1,0:T(8,128)(2,1)S(1)}, bf16[64,512]{1,0:T(8,128)(2,1)}, u32[]{:S(2)}) copy-start(bf16[64,512]{1,0:T(8,128)(2,1)} %rope_hbm.1) | copy-start | bytes 196612

commit v2 on v1

--- a/solution.py
+++ b/solution.py
@@ -244,9 +244,9 @@
         rope_wide[pl.ds(h, q_dev, stride=heads), :] = piece
     rope_queries[...] = rope_wide[:, :rope_width].astype(jnp.bfloat16)
 
-    tile = tile_rows(rows, 256)
-
-    def attend(places, first=False, key_base=None):
+    tile = tile_rows(rows, 512)
+
+    def attend(places, first=False, key_base=None, between=None, after=None):
         def key_rows():
             return jnp.concatenate([keys[b, r, j, :chunk, :] for b, r, j in places], axis=0)
 
@@ -308,29 +308,26 @@
                 attended[k, at, :] = piece
             row_max[at, :] = jnp.broadcast_to(top, (tile, lanes))
 
-        def body(step, _):
-            base = pl.multiple_of(step * (2 * tile), tile)
-            left = scores_of(base)
-            right = scores_of(base + tile)
-            fold(base, left)
-            fold(base + tile, right)
-            return 0
-
-        lax.fori_loop(0, rows // (2 * tile), body, 0)
-
-    def attend_share(b, k):
+        bases = list(range(0, rows, tile))
+        scores = [scores_of(base) for base in bases]
+        for n, base in enumerate(bases):
+            fold(base, scores[n])
+            if n == 0 and between is not None:
+                between()
+        if after is not None:
+            after()
+
+    def attend_shares(b, pieces, between=None):
         @pl.when(z >= 2 ** (b - 1))
         def _():
-            for i in range(per_share):
+            for k, i in pieces:
                 core_copy(b, k, i, sibling).wait_recv()
             attend(
-                [
-                    (b, r, share(k) * per_share + i)
-                    for r in (c, sibling)
-                    for i in range(per_share)
-                ]
-            )
-
+                [(b, r, share(k) * per_share + i) for r in (c, sibling) for k, i in pieces],
+                between=between,
+            )
+
+    others = range(1, n_head)
     attend([(0, c, j) for j in range(chunks)], first=True, key_base=c * half)
     send_on(1, 0)
     own_copy(sibling).wait_recv()
@@ -338,19 +335,25 @@
     for i in range(1, per_share):
         send_on(1, i)
     for b in range(1, levels + 1):
-        for k in range(1, n_head):
+        for k in others:
             pass_core(b, k, 0)
-        attend_share(b, 0)
+        ahead = [(k, 0) for k in others] if per_share > 1 else []
         if b < levels:
+            attend_shares(b, [(0, i) for i in range(per_share)])
             send_on(b + 1, 0)
-        for k in range(1, n_head):
-            for i in range(1, per_share):
-                pass_core(b, k, i)
-        for k in range(1, n_head):
-            attend_share(b, k)
-        if b < levels:
+            for k in others:
+                for i in range(1, per_share):
+                    pass_core(b, k, i)
+            attend_shares(b, [(k, i) for k in others for i in range(per_share)])
             for i in range(1, per_share):
                 send_on(b + 1, i)
+        else:
+            attend_shares(b, [(0, i) for i in range(per_share)] + ahead)
+            rest = [(k, i) for k in others for i in range(per_share) if (k, i) not in ahead]
+            for k, i in rest:
+                if i:
+                    pass_core(b, k, i)
+            attend_shares(b, rest)
 
     value_load.wait()
 
@@ -514,7 +517,7 @@
             dma((pieces, others)),
         ],
         compiler_params=pltpu.CompilerParams(
-            collective_id=0, has_side_effects=True, vmem_limit_bytes=50 * 1024 * 1024
+            collective_id=0, has_side_effects=True, vmem_limit_bytes=63 * 1024 * 1024
         ),
         cost_estimate=pl.CostEstimate(
             flops=2 * rows * (levels + 1) * 2 * half * (2 * width + rope_width),

time: 43.3 us -> 38.1 us (0.88)
  local copies, waits for them, and re-layouts: 5.92 us -> 1.64 us
  Pallas kernels: 37 us -> 36.3 us
    unnamed x11 -> x1, local copies, waits for them, and re-layouts: 5.92 us -> 1.64 us
    pallas_call x1, Pallas kernels: 37 us -> 36.3 us  [shards(): pl.pallas_call(functools.partial(kernel, dims), out_shape=jax.ShapeDtypeS...]
where the time goes in v2:
time: 38.1 us; the launch traced here: 38 us
  Pallas kernels  36.3 us (95%)
  local copies, waits for them, and re-layouts  1.64 us (4%)
    pallas_call x1, Pallas kernels, shards(): pl.pallas_call(functools.partial(kernel, dims), out_shape=jax.ShapeDtypeS...  36.3 us
    unnamed x1, local copies, waits for them, and re-layouts  1.64 us

profile of v2, /device:TPU:17, one launch (start us, length us, event | category | flops | bytes accessed | tf_op | source)
XLA Modules:
  0.0 38.0 jit_solution(13874934903266164332)
XLA Ops:
  0.0 36.3 %shard_map.64 = bf16[32,3584]{1,0:T(8,128)(2,1)} custom-call(bf16[128,8,512]{2,1,0:T(8,128)(2,1)} %query_hbm.1, bf16[128,512]{1,0:T(8,128)(2,1)} %query_rope_hbm.1, bf16[512,512]{1,0:T(8,128)(2,1)} %latent_hbm.1, bf16[64,512]{1,0:T(8,128)(2,1)} %rope_hbm.1, bf16[8,512,128]{2,1,0:T(8,128)(2,1)} %value_up_hbm.1, bf16[1024,3584]{1,0:T(8,128)(2,1)} %out_proj_hbm.1), custom_call_target="tpu_custom_call" | custom-call | flops 6845104128 | bytes 8388608 | tf_op jit(solution)/shard_map/pallas_call | solution.py:481
  36.3 1.6 %copy.8 = bf16[32,3584]{1,0:T(8,128)(2,1)} copy(bf16[32,3584]{1,0:T(8,128)(2,1)} %shard_map.64) | data formatting | bytes 458752

commit v3 on v2

--- a/solution.py
+++ b/solution.py
@@ -44,7 +44,7 @@
     out_proj,
     queries,
     rope_wide,
-    rope_queries,
+    keys_across,
     row_max,
     row_sum,
     attended,
@@ -197,15 +197,14 @@
         @pl.when(z >= 2 ** (b - 1))
         def _():
             seq_copy(b, i).wait_recv()
+            core_copy(b, 0, i, c).start()
+            for k in range(1, n_head):
+                head_copy(b, k, i).start()
             if b < levels:
 
                 @pl.when(seq_start(b + 1, i))
                 def _():
                     seq_copy(b + 1, i).start()
-
-            for k in range(1, n_head):
-                head_copy(b, k, i).start()
-            core_copy(b, 0, i, c).start()
 
     def pass_core(b, k, i):
         @pl.when(z >= 2 ** (b - 1))
@@ -213,28 +212,26 @@
             head_arrival(b, k, i).wait_recv()
             core_copy(b, k, i, c).start()
 
+    own_copy(c).start()
     for i in range(per_share):
 
         @pl.when(seq_start(1, i))
         def _():
             seq_copy(1, i).start()
-
-    own_copy(c).start()
 
     query_load.wait()
     query_rope_load.wait()
     if len(query_in.shape) == 3:
         step_q = q_dev // 4
         for part in range(4):
-            queries[part * step_q * heads : (part + 1) * step_q * heads, :] = (
+            queries[part * step_q * heads : (part + 1) * step_q * heads, :width] = (
                 query_in[part * step_q : (part + 1) * step_q]
                 .astype(jnp.float32)
                 .reshape(step_q * heads, width)
                 .astype(jnp.bfloat16)
             )
-        query_source = queries
     else:
-        query_source = query_in
+        queries[:, :width] = query_in[...]
     for h in range(heads):
         start = h * rope_width // lanes * lanes
         shift = h * rope_width - start
@@ -242,11 +239,11 @@
         if shift:
             piece = pltpu.roll(piece, lanes - shift, 1)
         rope_wide[pl.ds(h, q_dev, stride=heads), :] = piece
-    rope_queries[...] = rope_wide[:, :rope_width].astype(jnp.bfloat16)
+    queries[:, width:] = rope_wide[:, :rope_width].astype(jnp.bfloat16)
 
     tile = tile_rows(rows, 512)
 
-    def attend(places, first=False, key_base=None, between=None, after=None):
+    def attend(places, first=False, key_base=None, between=None):
         def key_rows():
             return jnp.concatenate([keys[b, r, j, :chunk, :] for b, r, j in places], axis=0)
 
@@ -265,16 +262,14 @@
                 axis=1,
             )
 
+        count = len(places) * chunk
+        keys_across[:width, :count] = key_rows().T
+        keys_across[width:, :count] = key_ropes()
+
         def scores_of(base):
             at = pl.ds(base, tile)
-            scores = lax.dot_general(
-                query_source[at, :],
-                key_rows(),
-                (((1,), (1,)), ((), ())),
-                preferred_element_type=jnp.float32,
-            )
-            scores = scores + jnp.dot(
-                rope_queries[at, :], key_ropes(), preferred_element_type=jnp.float32
+            scores = jnp.dot(
+                queries[at, :], keys_across[:, :count], preferred_element_type=jnp.float32
             )
             if key_base is not None:
                 key = key_base + lax.broadcasted_iota(jnp.int32, scores.shape, 1)
@@ -314,8 +309,6 @@
             fold(base, scores[n])
             if n == 0 and between is not None:
                 between()
-        if after is not None:
-            after()
 
     def attend_shares(b, pieces, between=None):
         @pl.when(z >= 2 ** (b - 1))
@@ -328,25 +321,35 @@
             )
 
     others = range(1, n_head)
+
+    def later_arrivals(b):
+        for i in range(1, per_share):
+            send_on(b, i)
+
     attend([(0, c, j) for j in range(chunks)], first=True, key_base=c * half)
     send_on(1, 0)
     own_copy(sibling).wait_recv()
-    attend([(0, sibling, j) for j in range(chunks)], key_base=sibling * half)
-    for i in range(1, per_share):
-        send_on(1, i)
+    attend(
+        [(0, sibling, j) for j in range(chunks)],
+        key_base=sibling * half,
+        between=lambda: later_arrivals(1),
+    )
     for b in range(1, levels + 1):
         for k in others:
             pass_core(b, k, 0)
         ahead = [(k, 0) for k in others] if per_share > 1 else []
         if b < levels:
-            attend_shares(b, [(0, i) for i in range(per_share)])
-            send_on(b + 1, 0)
+            attend_shares(
+                b, [(0, i) for i in range(per_share)], between=lambda: send_on(b + 1, 0)
+            )
             for k in others:
                 for i in range(1, per_share):
                     pass_core(b, k, i)
-            attend_shares(b, [(k, i) for k in others for i in range(per_share)])
-            for i in range(1, per_share):
-                send_on(b + 1, i)
+            attend_shares(
+                b,
+                [(k, i) for k in others for i in range(per_share)],
+                between=lambda: later_arrivals(b + 1),
+            )
         else:
             attend_shares(b, [(0, i) for i in range(per_share)] + ahead)
             rest = [(k, i) for k in others for i in range(per_share) if (k, i) not in ahead]
@@ -490,9 +493,9 @@
             pltpu.VMEM(key_rope.shape, bf16),
             pltpu.VMEM(value_up.shape, bf16),
             pltpu.VMEM(out_proj.shape, bf16),
-            pltpu.VMEM((rows, width), bf16),
+            pltpu.VMEM((rows, width + rope_width), bf16),
             pltpu.VMEM((rows, lanes), f32),
-            pltpu.VMEM((rows, rope_width), bf16),
+            pltpu.VMEM((width + rope_width, 2 * half), bf16),
             pltpu.VMEM((rows, lanes), f32),
             pltpu.VMEM((rows, lanes), f32),
             pltpu.VMEM((width // lanes, rows, lanes), f32),

time: 38.1 us -> 37.7 us (0.990)
  Pallas kernels: 36.3 us -> 35.9 us
    pallas_call x1, Pallas kernels: 36.3 us -> 35.9 us  [shards(): pl.pallas_call(functools.partial(kernel, dims), out_shape=jax.ShapeDtypeS...]
where the time goes in v3:
time: 37.7 us; the launch traced here: 37.5 us
  Pallas kernels  35.9 us (95%)
  local copies, waits for them, and re-layouts  1.64 us (4%)
    pallas_call x1, Pallas kernels, shards(): pl.pallas_call(functools.partial(kernel, dims), out_shape=jax.ShapeDtypeS...  35.9 us
    unnamed x1, local copies, waits for them, and re-layouts  1.64 us

profile of v3, /device:TPU:17, one launch (start us, length us, event | category | flops | bytes accessed | tf_op | source)
XLA Modules:
  0.0 37.5 jit_solution(4992729843173849745)
XLA Ops:
  0.0 35.9 %shard_map.64 = bf16[32,3584]{1,0:T(8,128)(2,1)} custom-call(bf16[128,8,512]{2,1,0:T(8,128)(2,1)} %query_hbm.1, bf16[128,512]{1,0:T(8,128)(2,1)} %query_rope_hbm.1, bf16[512,512]{1,0:T(8,128)(2,1)} %latent_hbm.1, bf16[64,512]{1,0:T(8,128)(2,1)} %rope_hbm.1, bf16[8,512,128]{2,1,0:T(8,128)(2,1)} %value_up_hbm.1, bf16[1024,3584]{1,0:T(8,128)(2,1)} %out_proj_hbm.1), custom_call_target="tpu_custom_call" | custom-call | flops 6845104128 | bytes 8388608 | tf_op jit(solution)/shard_map/pallas_call | solution.py:484
  35.9 1.6 %copy.8 = bf16[32,3584]{1,0:T(8,128)(2,1)} copy(bf16[32,3584]{1,0:T(8,128)(2,1)} %shard_map.64) | data formatting | bytes 458752

commit v4 on v3

--- a/solution.py
+++ b/solution.py
@@ -18,6 +18,11 @@
     while rows % tile:
         tile -= 8
     return tile
+
+
+def part_rows(chunk, pack):
+    first = chunk // 2
+    return ((0, first), (first, chunk + pack - first))
 
 
 def column_width(columns, most):
@@ -135,16 +140,19 @@
     def share(k):
         return lax.rem(x + n_head - k, n_head)
 
-    def place(b, r, k, i):
-        return keys.at[b, r, share(k) * per_share + i]
-
-    def seq_copy(b, i):
+    parts = part_rows(chunk, pack)
+
+    def place(b, r, k, i, part):
+        start, count = parts[part]
+        return keys.at[b, r, share(k) * per_share + i, pl.ds(start, count), :]
+
+    def seq_copy(b, i, part):
         hop = 1 if b == 1 else 2 ** (b - 2)
         return pltpu.make_async_remote_copy(
-            src_ref=place(b - 1, c, 0, i),
-            dst_ref=place(b, c, 0, i),
-            send_sem=seq_send.at[b - 1, i],
-            recv_sem=seq_recv.at[b - 1, i],
+            src_ref=place(b - 1, c, 0, i, part),
+            dst_ref=place(b, c, 0, i, part),
+            send_sem=seq_send.at[b - 1, i, part],
+            recv_sem=seq_recv.at[b - 1, i, part],
             device_id={"seq": jnp.minimum(z + hop, n_seq - 1)},
             device_id_type=MESH,
         )
@@ -153,32 +161,32 @@
         hop = 1 if b == 1 else 2 ** (b - 2)
         return (z + hop < n_seq) & (z >= (0 if b == 1 else 2 ** (b - 2)))
 
-    def head_copy(b, k, i):
-        return pltpu.make_async_remote_copy(
-            src_ref=place(b, c, 0, i),
-            dst_ref=place(b, c, 0, i),
-            send_sem=head_send.at[b - 1, k - 1, i],
-            recv_sem=head_recv.at[b - 1, k - 1, i],
+    def head_copy(b, k, i, part):
+        return pltpu.make_async_remote_copy(
+            src_ref=place(b, c, 0, i, part),
+            dst_ref=place(b, c, 0, i, part),
+            send_sem=head_send.at[b - 1, k - 1, i, part],
+            recv_sem=head_recv.at[b - 1, k - 1, i, part],
             device_id={"head": lax.rem(x + k, n_head)},
             device_id_type=MESH,
         )
 
-    def head_arrival(b, k, i):
-        return pltpu.make_async_remote_copy(
-            src_ref=place(b, c, k, i),
-            dst_ref=place(b, c, k, i),
-            send_sem=head_send.at[b - 1, k - 1, i],
-            recv_sem=head_recv.at[b - 1, k - 1, i],
+    def head_arrival(b, k, i, part):
+        return pltpu.make_async_remote_copy(
+            src_ref=place(b, c, k, i, part),
+            dst_ref=place(b, c, k, i, part),
+            send_sem=head_send.at[b - 1, k - 1, i, part],
+            recv_sem=head_recv.at[b - 1, k - 1, i, part],
             device_id={"head": lax.rem(x + k, n_head)},
             device_id_type=MESH,
         )
 
-    def core_copy(b, k, i, r):
-        return pltpu.make_async_remote_copy(
-            src_ref=place(b, r, k, i),
-            dst_ref=place(b, r, k, i),
-            send_sem=core_send.at[b - 1, k, i],
-            recv_sem=core_recv.at[b - 1, k, i],
+    def core_copy(b, k, i, r, part):
+        return pltpu.make_async_remote_copy(
+            src_ref=place(b, r, k, i, part),
+            dst_ref=place(b, r, k, i, part),
+            send_sem=core_send.at[b - 1, k, i, part],
+            recv_sem=core_recv.at[b - 1, k, i, part],
             device_id={"rep": sibling},
             device_id_type=MESH,
         )
@@ -196,28 +204,32 @@
     def send_on(b, i):
         @pl.when(z >= 2 ** (b - 1))
         def _():
-            seq_copy(b, i).wait_recv()
-            core_copy(b, 0, i, c).start()
-            for k in range(1, n_head):
-                head_copy(b, k, i).start()
-            if b < levels:
-
-                @pl.when(seq_start(b + 1, i))
-                def _():
-                    seq_copy(b + 1, i).start()
+            for part in range(len(parts)):
+                seq_copy(b, i, part).wait_recv()
+                for k in range(1, n_head):
+                    head_copy(b, k, i, part).start()
+                if b < levels:
+
+                    @pl.when(seq_start(b + 1, i))
+                    def _():
+                        seq_copy(b + 1, i, part).start()
+
+                core_copy(b, 0, i, c, part).start()
 
     def pass_core(b, k, i):
         @pl.when(z >= 2 ** (b - 1))
         def _():
-            head_arrival(b, k, i).wait_recv()
-            core_copy(b, k, i, c).start()
+            for part in range(len(parts)):
+                head_arrival(b, k, i, part).wait_recv()
+                core_copy(b, k, i, c, part).start()
 
     own_copy(c).start()
     for i in range(per_share):
 
         @pl.when(seq_start(1, i))
         def _():
-            seq_copy(1, i).start()
+            for part in range(len(parts)):
+                seq_copy(1, i, part).start()
 
     query_load.wait()
     query_rope_load.wait()
@@ -314,7 +326,8 @@
         @pl.when(z >= 2 ** (b - 1))
         def _():
             for k, i in pieces:
-                core_copy(b, k, i, sibling).wait_recv()
+                for part in range(len(parts)):
+                    core_copy(b, k, i, sibling, part).wait_recv()
             attend(
                 [(b, r, share(k) * per_share + i) for r in (c, sibling) for k, i in pieces],
                 between=between,
@@ -445,14 +458,16 @@
 
             @pl.when(seq_start(b, i))
             def _():
-                seq_copy(b, i).wait_send()
+                for part in range(len(parts)):
+                    seq_copy(b, i, part).wait_send()
 
             @pl.when(z >= 2 ** (b - 1))
             def _():
-                for k in range(1, n_head):
-                    head_copy(b, k, i).wait_send()
-                for k in range(n_head):
-                    core_copy(b, k, i, c).wait_send()
+                for part in range(len(parts)):
+                    for k in range(1, n_head):
+                        head_copy(b, k, i, part).wait_send()
+                    for k in range(n_head):
+                        core_copy(b, k, i, c, part).wait_send()
 
     for piece in range(pieces):
         sum_core(piece).wait_send()
@@ -508,12 +523,12 @@
             dma((chunks + 5,)),
             dma,
             dma,
-            dma((levels, per_share)),
-            dma((levels, per_share)),
-            dma((levels, others, per_share)),
-            dma((levels, others, per_share)),
-            dma((levels, n_head, per_share)),
-            dma((levels, n_head, per_share)),
+            dma((levels, per_share, 2)),
+            dma((levels, per_share, 2)),
+            dma((levels, others, per_share, 2)),
+            dma((levels, others, per_share, 2)),
+            dma((levels, n_head, per_share, 2)),
+            dma((levels, n_head, per_share, 2)),
             dma((pieces,)),
             dma((pieces,)),
             dma((pieces, others)),

time: 37.7 us -> 37.5 us (level)
  Pallas kernels: 35.9 us -> 35.5 us
    pallas_call x1, Pallas kernels: 35.9 us -> 35.5 us  [shards(): pl.pallas_call(functools.partial(kernel, dims), out_shape=jax.ShapeDtypeS...]
where the time goes in v4:
time: 37.5 us; the launch traced here: 37.2 us
  Pallas kernels  35.5 us (95%)
  local copies, waits for them, and re-layouts  1.64 us (4%)
    pallas_call x1, Pallas kernels, shards(): pl.pallas_call(functools.partial(kernel, dims), out_shape=jax.ShapeDtypeS...  35.5 us
    unnamed x1, local copies, waits for them, and re-layouts  1.64 us

profile of v4, /device:TPU:17, one launch (start us, length us, event | category | flops | bytes accessed | tf_op | source)
XLA Modules:
  0.0 37.2 jit_solution(2690706401926575483)
XLA Ops:
  0.0 35.5 %shard_map.64 = bf16[32,3584]{1,0:T(8,128)(2,1)} custom-call(bf16[128,8,512]{2,1,0:T(8,128)(2,1)} %query_hbm.1, bf16[128,512]{1,0:T(8,128)(2,1)} %query_rope_hbm.1, bf16[512,512]{1,0:T(8,128)(2,1)} %latent_hbm.1, bf16[64,512]{1,0:T(8,128)(2,1)} %rope_hbm.1, bf16[8,512,128]{2,1,0:T(8,128)(2,1)} %value_up_hbm.1, bf16[1024,3584]{1,0:T(8,128)(2,1)} %out_proj_hbm.1), custom_call_target="tpu_custom_call" | custom-call | flops 6845104128 | bytes 8388608 | tf_op jit(solution)/shard_map/pallas_call | solution.py:499
  35.5 1.6 %copy.8 = bf16[32,3584]{1,0:T(8,128)(2,1)} copy(bf16[32,3584]{1,0:T(8,128)(2,1)} %shard_map.64) | data formatting | bytes 458752
